TPU v7x, 32 devices: a whole 2x2x4 slice. The times are simulated.
32 devices in a mesh: group: 2 (over y), expert: 4 (over z), req: 4 (over x, core).
Axes of the slice: x: 2, y: 2, z: 4, core: 2. Of those that a mesh axis runs over, the one named last changes fastest.
Arguments:
- verify_in: bfloat16 [128, 4096], P(('group', 'expert'), 'req'), parts along dimension 0, may hold values from -6 to 6
- expert_ids: int32 [128, 2], P(('group', 'expert')), parts along dimension 0, may hold values from 0 to 7, all different within a row; in each aligned block of 16 rows (0 to 15, 16 to 31, ...) at most 8 rows name the same one
- gate_weights: float32 [128, 2], P(('group', 'expert')), parts along dimension 0, may hold values from 0.2 to 1
- moe_gate: bfloat16 [32, 4096, 1792], P('expert', None, 'req'), may hold values from -0.09375 to 0.09375
- moe_up: bfloat16 [32, 4096, 1792], P('expert', None, 'req'), may hold values from -0.09375 to 0.09375
- moe_down: bfloat16 [32, 1792, 4096], P('expert', 'req'), may hold values from -0.09375 to 0.09375
- draft_emb: bfloat16 [2048, 4096], P(('group', 'req'), 'expert'), parts along dimension 0, may hold values from -6 to 6
- draft_feat: bfloat16 [2048, 4096], P(('group', 'req'), 'expert'), parts along dimension 0, may hold values from -18 to 18
- parents: int32 [2048], P(('group', 'req')), parts along dimension 0, may hold values from 0 to 1023, as said below
- join_weight: bfloat16 [8192, 4096], P('req', 'expert'), may hold values from -3 to 3
- norm_gain: float32 [4096], P('expert'), may hold values from 0.5 to 1.5
- draft_gate: bfloat16 [4096, 7168], P('req', 'expert'), may hold values from -0.09375 to 0.09375
- draft_up: bfloat16 [4096, 7168], P('req', 'expert'), may hold values from -0.09375 to 0.09375
- draft_down: bfloat16 [7168, 4096], P('expert', 'req'), may hold values from -0.09375 to 0.09375
Outputs:
- verify_out: bfloat16 [128, 4096], P(('group', 'expert'), 'req'), parts along dimension 0
- draft_out: bfloat16 [2048, 4096], P(('group', 'req'), 'expert'), parts along dimension 0
There are 2 independent parts, one for each index of `group`. A program takes and returns all parts, laid end to end along the dimension named above; an argument that names none is the same for every part. Nothing has to cross between parts.
Inputs may be any that keep to these rules, and one draw needn't show every extreme that they name: `expert_ids`: each row names two different experts; within the rows of one index of expert, no expert is named more than 8 times. `parents`: each row's parent is a row of the same tree of 64 consecutive rows at an earlier position; a tree's first row is its own parent.
All inputs are finite; a program needn't handle non-finite values.
Results may differ from a plain program's by a relative error of at most 0.015.
Values may be sent and summed in bfloat16 or wider, within the bound.
A program may use at most 256 MiB of HBM per device.

v0:
```python
import functools

import jax
import jax.numpy as jnp
from jax import lax
from jax.experimental import pallas as pl
from jax.experimental.pallas import tpu as pltpu
from jax.sharding import PartitionSpec as P

EXPERTS = 8
EPS = 1e-05


def verify_layer(verify_in, expert_ids, gate_weights, moe_gate, moe_up, moe_down):
    n_expert, n_req = lax.axis_size("expert"), lax.axis_size("req")
    own_rows, own_width = verify_in.shape
    local = moe_gate.shape[0]
    slices = local * n_expert // EXPERTS
    rows, width = own_rows * n_expert, own_width * n_req

    blocks = lax.all_gather(verify_in, ("expert", "req"), axis=0)
    blocks = blocks.reshape(n_expert, n_req, own_rows, own_width)
    hidden_in = blocks.transpose(0, 2, 1, 3).reshape(rows, width)
    routes = jnp.concatenate([expert_ids.astype(jnp.float32), gate_weights], axis=1)
    routes = lax.all_gather(routes, "expert", axis=0, tiled=True)
    top = expert_ids.shape[1]
    ids, gains = routes[:, :top].astype(jnp.int32), routes[:, top:]
    held = (lax.axis_index("expert") * local + jnp.arange(local, dtype=jnp.int32)) // slices
    mixing = jnp.sum(
        jnp.where(ids[None] == held[:, None, None], gains[None], 0.0), axis=2
    )

    batch = jnp.broadcast_to(hidden_in[None], (local, rows, width))
    gate = jnp.einsum("kmd,kdf->kmf", batch, moe_gate, preferred_element_type=jnp.float32)
    up = jnp.einsum("kmd,kdf->kmf", batch, moe_up, preferred_element_type=jnp.float32)
    hidden = (jax.nn.silu(gate) * up * mixing[:, :, None]).astype(jnp.bfloat16)
    hidden = hidden.transpose(1, 0, 2).reshape(rows, -1)
    down = moe_down.reshape(-1, width)
    partial = jnp.dot(hidden, down, preferred_element_type=jnp.float32).astype(jnp.bfloat16)
    partial = partial.reshape(n_expert, own_rows, n_req, own_width).transpose(0, 2, 1, 3)
    partial = partial.reshape(n_expert * n_req, own_rows, own_width)
    out = lax.psum_scatter(partial, ("expert", "req"), scatter_dimension=0)
    return out.astype(jnp.bfloat16)


def draft_step(
    draft_emb, draft_feat, parents, join_weight, norm_gain, draft_gate, draft_up, draft_down
):
    n_expert, n_req = lax.axis_size("expert"), lax.axis_size("req")
    n_group = lax.axis_size("group")
    r, g = lax.axis_index("req"), lax.axis_index("group")
    half = n_req // 2
    side, place = r // half, r % half
    rows, width = draft_emb.shape[0], draft_emb.shape[1] * n_expert

    def across(x):
        return lax.ppermute(x, "req", [(i, (i + half) % n_req) for i in range(n_req)])

    def within(x, step):
        return lax.ppermute(
            x,
            "req",
            [(i // half * half + (i + step) % half, i) for i in range(n_req)],
        )

    def other_group(x, step):
        return lax.ppermute(x, "group", [((i + step) % n_group, i) for i in range(n_group)])

    def pieces_of(weight):
        found = [(side * half + (place + s) % half, None, weight if s == 0 else within(weight, s))
                 for s in range(half)]
        depth = weight.shape[0] // n_group
        part = lax.dynamic_slice_in_dim(weight, g * depth, depth, axis=0)
        crossed = across(part)
        far = [(g, crossed)]
        far += [((g + s) % n_group, other_group(crossed, s)) for s in range(1, n_group)]
        for s in range(half):
            index = (1 - side) * half + (place + s) % half
            found += [(index, p, a if s == 0 else within(a, s)) for p, a in far]
        return found

    local_parent = parents - r * rows
    feat = jnp.take(draft_feat, local_parent, axis=0)
    mine = jnp.where(side == 0, draft_emb, feat)
    theirs = across(jnp.where(side == 0, feat, draft_emb))
    join_pieces = [
        ((place + s) % half, join_weight if s == 0 else within(join_weight, s))
        for s in range(half)
    ]
    depth = join_weight.shape[0]

    def join(block):
        whole = lax.all_gather(block, "expert", axis=1, tiled=True)
        return sum(
            jnp.dot(
                lax.dynamic_slice_in_dim(whole, index * depth, depth, axis=1),
                weight,
                preferred_element_type=jnp.float32,
            )
            for index, weight in join_pieces
        )

    kept = join(mine)
    sent = join(theirs)
    joined_state = kept + across(sent.astype(jnp.bfloat16)).astype(jnp.float32)

    squares = lax.psum(jnp.sum(joined_state * joined_state, axis=1), "expert")
    scale = lax.rsqrt(squares[:, None] / width + EPS)
    scaled = (joined_state * norm_gain[None, :]).astype(jnp.bfloat16)
    inputs = lax.all_gather(scaled, "expert", axis=1, tiled=True)

    def project(weight):
        total = 0.0
        full = weight.shape[0]
        for index, part, array in pieces_of(weight):
            start = index * full if part is None else index * full + part * array.shape[0]
            columns = lax.dynamic_slice_in_dim(inputs, start, array.shape[0], axis=1)
            total += jnp.dot(columns, array, preferred_element_type=jnp.float32)
        return total

    gate = project(draft_gate) * scale
    up = project(draft_up) * scale
    hidden = (jax.nn.silu(gate) * up).astype(jnp.bfloat16)

    near, far = [], []
    full = draft_down.shape[0]
    pieces = pieces_of(draft_down)
    for s in range(half):
        near.append(jnp.dot(hidden, pieces[s][2], preferred_element_type=jnp.float32))
    for s in range(half):
        total = 0.0
        for _, part, array in pieces[half + s * n_group : half + (s + 1) * n_group]:
            columns = lax.dynamic_slice_in_dim(hidden, part * array.shape[0], array.shape[0], axis=1)
            total += jnp.dot(columns, array, preferred_element_type=jnp.float32)
        far.append(total)

    def ordered(blocks):
        stack = jnp.stack(blocks).astype(jnp.bfloat16)
        order = (jnp.arange(half) - place) % half
        return stack[order]

    near, far = ordered(near), ordered(far)
    both = jnp.where(side == 0, jnp.concatenate([near, far]), jnp.concatenate([far, near]))
    terms = both.transpose(1, 0, 2).reshape(rows, width)
    mlp_sum = lax.psum_scatter(terms, "expert", scatter_dimension=1, tiled=True)
    return (joined_state + mlp_sum.astype(jnp.float32)).astype(jnp.bfloat16)


def front_kernel(
    shape,
    mine_ref, theirs_ref, gain_ref, rows_ref, routes_ref,
    join_ref, gate_ref, up_ref, down_ref, moe_gate_ref, moe_up_ref, moe_down_ref,
    state_ref, verify_ref, squares_ref, scaled_ref,
    gate_sib, up_sib, down_sib, gate_far, up_far, down_far, gate_sibfar, up_sibfar, down_sibfar,
    near_all, far_all, near_acc, sent_acc, swap_out, swap_in, join_all, square_buf, scaled_buf,
    row_all, route_all, gate_buf, up_buf, down_buf, moe_acc, moe_out, moe_in, merged_out, merged_in,
    ring_send_r, ring_send_l, ring_recv, misc_send, misc_recv, local_sem, moe_sem,
    mate_send, mate_recv, wide_send, wide_recv,
):
    n_expert, n_req, n_group, slices = shape
    half = n_req // 2
    g, e, r = lax.axis_index("group"), lax.axis_index("expert"), lax.axis_index("req")
    place = lax.rem(r, half)
    sib = r + 1 - 2 * place
    partner = lax.rem(r + half, n_req)

    def remote(src, dst, send, recv, **where):
        return pltpu.make_async_remote_copy(
            src_ref=src, dst_ref=dst, send_sem=send, recv_sem=recv,
            device_id=where, device_id_type=pl.DeviceIdType.MESH,
        )

    barrier = pltpu.get_barrier_semaphore()
    for s in range(1, n_req):
        pl.semaphore_signal(barrier, inc=1, device_id={"req": lax.rem(r + s, n_req)},
                            device_id_type=pl.DeviceIdType.MESH)
    for s in range(1, n_expert):
        pl.semaphore_signal(barrier, inc=1, device_id={"expert": lax.rem(e + s, n_expert)},
                            device_id_type=pl.DeviceIdType.MESH)
    pl.semaphore_signal(barrier, inc=1, device_id={"group": 1 - g},
                        device_id_type=pl.DeviceIdType.MESH)

    local = moe_gate_ref.shape[0]

    def fetch(k, slot):
        return [
            pltpu.make_async_copy(w.at[k], b.at[slot], moe_sem.at[i, slot])
            for i, (w, b) in enumerate(
                ((moe_gate_ref, gate_buf), (moe_up_ref, up_buf), (moe_down_ref, down_buf)))
        ]

    for c in fetch(0, 0):
        c.start()
    own_join = pltpu.make_async_copy(join_ref, join_all.at[place], local_sem.at[0])
    own_join.start()
    own_width = rows_ref.shape[1]
    own_columns = pl.ds(pl.multiple_of(r * own_width, own_width), own_width)
    near_all[e] = mine_ref[...]
    row_all[e, :, own_columns] = rows_ref[...]
    route_all[e] = routes_ref[...]
    pl.semaphore_wait(barrier, n_req + n_expert - 1)

    def to_right(i, buf, b):
        return remote(buf.at[b], buf.at[b], ring_send_r.at[i, b], ring_recv.at[i, b],
                      expert=lax.rem(e + 1, n_expert))

    def to_left(i, buf, b):
        return remote(buf.at[b], buf.at[b], ring_send_l.at[i, b], ring_recv.at[i, b],
                      expert=lax.rem(e + n_expert - 1, n_expert))

    def ring_start(i, buf):
        @pl.when(e < n_expert - 1)
        def _():
            to_right(i, buf, e).start()

        @pl.when(e > 0)
        def _():
            to_left(i, buf, e).start()

    def ring_step(i, buf, s):
        @pl.when(e >= s)
        def _():
            to_right(i, buf, e - s).wait_recv()

            @pl.when(e < n_expert - 1)
            def _():
                to_right(i, buf, e - s).start()

        @pl.when(e + s < n_expert)
        def _():
            to_left(i, buf, e + s).wait_recv()

            @pl.when(e > 0)
            def _():
                to_left(i, buf, e + s).start()

    def ring_finish(i, buf):
        for b in range(n_expert):
            @pl.when((b <= e) & (e < n_expert - 1))
            def _():
                to_right(i, buf, b).wait_send()

            @pl.when((b >= e) & (e > 0))
            def _():
                to_left(i, buf, b).wait_send()

    def mates(buf_of, dst_of, row, axis, me, n):
        copies = []
        for s in range(1, n):
            mate = lax.rem(me + s, n)
            c = remote(buf_of(mate), dst_of, mate_send.at[row, s], mate_recv.at[row, s], **{axis: mate})
            c.start()
            copies.append(c)
        return copies

    cross = remote(theirs_ref, far_all.at[e], misc_send.at[0], misc_recv.at[0], req=partner)
    cross.start()
    rows_req = mates(lambda m: rows_ref, row_all.at[e, :, own_columns], 0, "req", r, n_req)
    routes_out = mates(lambda m: routes_ref, route_all.at[e], 1, "expert", e, n_expert)
    ring_start(0, near_all)
    join_out = remote(join_ref, join_all.at[place], misc_send.at[1], misc_recv.at[1], req=sib)
    join_out.start()
    for c in rows_req:
        c.wait_recv()
    rows_exp = mates(lambda m: row_all.at[e], row_all.at[e], 2, "expert", e, n_expert)
    sib_out = []
    for i, (w, d) in enumerate(((gate_ref, gate_sib), (up_ref, up_sib), (down_ref, down_sib))):
        c = remote(w, d, misc_send.at[2 + i], misc_recv.at[2 + i], req=sib)
        c.start()
        sib_out.append(c)

    weights = ((gate_ref, gate_far, gate_sibfar), (up_ref, up_far, up_sibfar), (down_ref, down_far, down_sibfar))
    cuts = 2
    chunks = []
    for own, far, sibfar in weights:
        part = own.shape[0] // n_group
        piece = part // cuts
        for cut in range(cuts):
            chunks.append((own, far, sibfar, part, piece, cut * piece))

    def span(c, owner):
        _, _, _, part, piece, start = chunks[c]
        return pl.ds(pl.multiple_of(owner * part + start, 16), piece)

    def over_req(c):
        at = span(c, g)
        return remote(chunks[c][0].at[at], chunks[c][1].at[at], wide_send.at[0, c], wide_recv.at[0, c], req=partner)

    def over_group(c):
        at = span(c, g)
        return remote(chunks[c][1].at[at], chunks[c][1].at[at], wide_send.at[1, c], wide_recv.at[1, c], group=1 - g)

    def to_sib(c, which):
        at = span(c, g if which == 2 else 1 - g)
        return remote(chunks[c][1].at[at], chunks[c][2].at[at], wide_send.at[which, c], wide_recv.at[which, c], req=sib)

    count = len(chunks)

    def relay(c):
        over_req(c).wait_recv()
        if c + 2 < count:
            over_req(c + 2).start()
        over_group(c).start()
        to_sib(c, 2).start()
        if c > 0:
            relay_last(c - 1)

    def relay_last(c):
        over_group(c).wait_recv()
        to_sib(c, 3).start()

    cross.wait_recv()
    ring_start(1, far_all)
    over_req(0).start()
    over_req(1).start()
    ring_step(0, near_all, 1)
    for c in rows_exp + routes_out:
        c.wait_recv()
    moe_acc[...] = jnp.zeros_like(moe_acc)
    own_rows = rows_ref.shape[0]
    rows = own_rows * n_expert

    def expert_piece(k, carry):
        slot = lax.rem(k, 2)

        @pl.when(k + 1 < local)
        def _():
            for c in fetch(k + 1, 1 - slot):
                c.start()

        for c in fetch(k, slot):
            c.wait()
        x = row_all[...].reshape(rows, row_all.shape[2])
        routes = route_all[...].reshape(rows, route_all.shape[2])
        expert = ((e * local + k) // slices).astype(jnp.float32)
        mixing = jnp.where(routes[:, 0:1] == expert, routes[:, 2:3], 0.0)
        mixing += jnp.where(routes[:, 1:2] == expert, routes[:, 3:4], 0.0)
        a = jnp.dot(x, gate_buf[slot], preferred_element_type=jnp.float32)
        b = jnp.dot(x, up_buf[slot], preferred_element_type=jnp.float32)
        hidden = (a / (1.0 + jnp.exp(-a)) * b * mixing).astype(jnp.bfloat16)
        moe_acc[...] += jnp.dot(hidden, down_buf[slot], preferred_element_type=jnp.float32)
        return carry

    def moe(start, stop):
        lax.fori_loop(start, stop, expert_piece, 0)

    quarter = local // 4
    moe(0, quarter)
    ring_step(0, near_all, 2)
    ring_step(1, far_all, 1)
    moe(quarter, 2 * quarter)
    relay(0)
    ring_step(0, near_all, 3)
    moe(2 * quarter, 3 * quarter)
    ring_step(1, far_all, 2)
    moe(3 * quarter, local)
    relay(1)

    moe_out[...] = moe_acc[...].astype(jnp.bfloat16).reshape(moe_out.shape)
    merge_exp = mates(lambda m: moe_out.at[m], moe_in.at[e], 3, "expert", e, n_expert)

    own_join.wait()
    join_out.wait_recv()
    block = near_all.shape[2]
    per = join_ref.shape[0] // block
    tile = 256

    def join(buf, acc):
        for n in range(acc.shape[1] // tile):
            at = pl.ds(n * tile, tile)
            total = 0.0
            for b in range(n_expert):
                w = join_all[b // per, pl.ds(b % per * block, block), at]
                total += jnp.dot(buf[b], w, preferred_element_type=jnp.float32)
            acc[:, at] = total

    join(near_all, near_acc)
    ring_step(1, far_all, 3)
    join(far_all, sent_acc)
    swap_out[...] = sent_acc[...].astype(jnp.bfloat16)
    swap = remote(swap_out, swap_in, misc_send.at[5], misc_recv.at[5], req=partner)
    swap.start()

    for c in merge_exp:
        c.wait_recv()
    merged = moe_out[e].astype(jnp.float32)
    for s in range(1, n_expert):
        merged += moe_in[lax.rem(e + n_expert - s, n_expert)].astype(jnp.float32)
    for j in range(n_req):
        merged_out[j] = merged[:, j * own_width:(j + 1) * own_width].astype(jnp.bfloat16)
    merge_req = mates(lambda m: merged_out.at[m], merged_in.at[r], 4, "req", r, n_req)

    swap.wait_recv()
    state = near_acc[...] + swap_in[...].astype(jnp.float32)
    state_ref[...] = state
    scaled_buf[e] = (state * gain_ref[...]).astype(jnp.bfloat16)
    ring_start(2, scaled_buf)
    lane = lax.broadcasted_iota(jnp.int32, (128, 128), 1)
    line = lax.broadcasted_iota(jnp.int32, (128, 128), 0)
    sums = jnp.sum(state * state, axis=1, keepdims=True)
    for j in range(state.shape[0] // 128):
        picked = jnp.where(lane == line, sums[j * 128:(j + 1) * 128], 0.0)
        square_buf[e, j:j + 1, :] = jnp.sum(picked, axis=0, keepdims=True)
    squares_out = mates(lambda m: square_buf.at[e], square_buf.at[e], 5, "expert", e, n_expert)

    for c in merge_req:
        c.wait_recv()
    out = merged_out[r].astype(jnp.float32)
    for s in range(1, n_req):
        out += merged_in[lax.rem(r + n_req - s, n_req)].astype(jnp.float32)
    verify_ref[...] = out.astype(jnp.bfloat16)

    relay(2)
    ring_step(2, scaled_buf, 1)
    relay(3)
    ring_step(2, scaled_buf, 2)
    relay(4)
    ring_step(2, scaled_buf, 3)
    for c in squares_out:
        c.wait_recv()
    squares_ref[...] = square_buf[...]
    keep = pltpu.make_async_copy(scaled_buf, scaled_ref, local_sem.at[1])
    keep.start()
    relay(5)
    relay_last(count - 1)
    keep.wait()

    for c in rows_req + routes_out + rows_exp + merge_exp + merge_req + squares_out + sib_out:
        c.wait_send()
    for c in (cross, join_out, swap):
        c.wait_send()
    for c in sib_out:
        c.wait_recv()
    for i, buf in enumerate((near_all, far_all, scaled_buf)):
        ring_finish(i, buf)
    for c in range(count):
        over_req(c).wait_send()
        over_group(c).wait_send()
        to_sib(c, 2).wait()
        to_sib(c, 3).wait()


def front(
    mine, theirs, gain, verify_in, routes, join_weight, draft_gate, draft_up, draft_down,
    moe_gate, moe_up, moe_down,
):
    n_expert, n_req, n_group = (lax.axis_size(a) for a in ("expert", "req", "group"))
    local, width, ff = moe_gate.shape
    slices = local * n_expert // EXPERTS
    rows, block = mine.shape
    own_rows, own_width = verify_in.shape
    bf, f32 = jnp.bfloat16, jnp.float32
    vmem, hbm = pl.BlockSpec(memory_space=pltpu.VMEM), pl.BlockSpec(memory_space=pl.ANY)
    weights = (draft_gate, draft_up, draft_down)
    like = [jax.ShapeDtypeStruct(w.shape, w.dtype) for w in weights]
    dma = pltpu.SemaphoreType.DMA
    n_chunks = 6
    big = max(n_expert, n_req)
    return pl.pallas_call(
        functools.partial(front_kernel, (n_expert, n_req, n_group, slices)),
        out_shape=[
            jax.ShapeDtypeStruct((rows, block), f32),
            jax.ShapeDtypeStruct(verify_in.shape, bf),
            jax.ShapeDtypeStruct((n_expert, 8, 128), f32),
            jax.ShapeDtypeStruct((n_expert, rows, block), bf),
            *like, *like, *like,
        ],
        in_specs=[vmem] * 5 + [hbm] * 7,
        out_specs=[vmem] * 3 + [hbm] * 10,
        scratch_shapes=[
            pltpu.VMEM((n_expert, rows, block), bf),
            pltpu.VMEM((n_expert, rows, block), bf),
            pltpu.VMEM((rows, block), f32),
            pltpu.VMEM((rows, block), f32),
            pltpu.VMEM((rows, block), bf),
            pltpu.VMEM((rows, block), bf),
            pltpu.VMEM((n_req // 2, *join_weight.shape), bf),
            pltpu.VMEM((n_expert, 8, 128), f32),
            pltpu.VMEM((n_expert, rows, block), bf),
            pltpu.VMEM((n_expert, own_rows, width), bf),
            pltpu.VMEM((n_expert, *routes.shape), f32),
            pltpu.VMEM((2, width, ff), bf),
            pltpu.VMEM((2, width, ff), bf),
            pltpu.VMEM((2, ff, width), bf),
            pltpu.VMEM((n_expert * own_rows, width), f32),
            pltpu.VMEM((n_expert, own_rows, width), bf),
            pltpu.VMEM((n_expert, own_rows, width), bf),
            pltpu.VMEM((n_req, own_rows, own_width), bf),
            pltpu.VMEM((n_req, own_rows, own_width), bf),
            dma((3, n_expert)), dma((3, n_expert)), dma((3, n_expert)),
            dma((6,)), dma((6,)), dma((2,)), dma((3, 2)),
            dma((6, big)), dma((6, big)), dma((4, n_chunks)), dma((4, n_chunks)),
        ],
        compiler_params=pltpu.CompilerParams(
            collective_id=0, has_side_effects=True, vmem_limit_bytes=56 * 2**20
        ),
        name="front",
    )(mine, theirs, gain, verify_in, routes, join_weight, *weights, moe_gate, moe_up, moe_down)


def fused(
    verify_in, expert_ids, gate_weights, moe_gate, moe_up, moe_down,
    draft_emb, draft_feat, parents, join_weight, norm_gain, draft_gate, draft_up, draft_down,
):
    n_expert, n_req = lax.axis_size("expert"), lax.axis_size("req")
    r = lax.axis_index("req")
    half = n_req // 2
    side, place = r // half, r % half
    rows, width = draft_emb.shape[0], draft_emb.shape[1] * n_expert
    feat = jnp.take(draft_feat, parents - r * rows, axis=0)
    mine = jnp.where(side == 0, draft_emb, feat)
    theirs = jnp.where(side == 0, feat, draft_emb)
    routes = jnp.concatenate([expert_ids.astype(jnp.float32), gate_weights], axis=1)
    routes = jnp.pad(routes, ((0, 0), (0, 128 - routes.shape[1])))
    state, verify_out, squares, inputs, *moved = front(
        mine, theirs, norm_gain[None, :], verify_in, routes, join_weight,
        draft_gate, draft_up, draft_down, moe_gate, moe_up, moe_down,
    )
    squares = jnp.sum(squares, axis=0).reshape(-1)[:rows]
    scale = lax.rsqrt(squares[:, None] / width + EPS)
    sib, partner = side * half + (1 - place), (r + half) % n_req
    sibfar = partner + 1 - 2 * place
    places = (r, sib, partner, sibfar)
    per_gate, per_up, per_down = (
        [w, moved[i], moved[3 + i], moved[6 + i]]
        for i, w in enumerate((draft_gate, draft_up, draft_down))
    )
    columns = [lax.dynamic_index_in_dim(inputs, p, 0, keepdims=False) for p in places]

    def project(shards):
        return scale * sum(
            jnp.dot(c, w, preferred_element_type=jnp.float32) for c, w in zip(columns, shards)
        )

    hidden = (jax.nn.silu(project(per_gate)) * project(per_up)).astype(jnp.bfloat16)
    near0, near1, far0, far1 = (
        jnp.dot(hidden, w, preferred_element_type=jnp.float32).astype(jnp.bfloat16)
        for w in per_down
    )
    n0, n1 = jnp.where(place == 0, near0, near1), jnp.where(place == 0, near1, near0)
    f0, f1 = jnp.where(place == 0, far0, far1), jnp.where(place == 0, far1, far0)
    first = jnp.where(side == 0, n0, f0), jnp.where(side == 0, n1, f1)
    second = jnp.where(side == 0, f0, n0), jnp.where(side == 0, f1, n1)
    terms = jnp.concatenate([*first, *second], axis=1)
    mlp_sum = lax.psum_scatter(terms, "expert", scatter_dimension=1, tiled=True)
    return (verify_out, (state + mlp_sum.astype(jnp.float32)).astype(jnp.bfloat16))


def per_device(
    verify_in,
    expert_ids,
    gate_weights,
    moe_gate,
    moe_up,
    moe_down,
    draft_emb,
    draft_feat,
    parents,
    join_weight,
    norm_gain,
    draft_gate,
    draft_up,
    draft_down,
):
    n_expert, n_req = lax.axis_size("expert"), lax.axis_size("req")
    block, rows = draft_emb.shape[1], draft_emb.shape[0]
    fits = (
        n_req == 4 and lax.axis_size("group") == 2 and n_expert == 4
        and join_weight.shape[0] % block == 0 and draft_gate.shape[0] == block
        and block % 256 == 0 and draft_gate.shape[1] % 128 == 0
        and rows % 128 == 0 and rows <= 1024 and expert_ids.shape[1] == 2
        and moe_gate.shape[0] % 4 == 0 and draft_down.shape[0] % 64 == 0
    )
    if fits:
        return fused(
            verify_in, expert_ids, gate_weights, moe_gate, moe_up, moe_down,
            draft_emb, draft_feat, parents, join_weight, norm_gain,
            draft_gate, draft_up, draft_down,
        )
    draft_out = draft_step(
        draft_emb, draft_feat, parents, join_weight, norm_gain, draft_gate, draft_up, draft_down
    )
    verify_out = verify_layer(verify_in, expert_ids, gate_weights, moe_gate, moe_up, moe_down)
    return (verify_out, draft_out)


def solution(mesh):
    in_specs = (
        P(("group", "expert"), "req"),
        P(("group", "expert"), None),
        P(("group", "expert"), None),
        P("expert", None, "req"),
        P("expert", None, "req"),
        P("expert", "req", None),
        P(("group", "req"), "expert"),
        P(("group", "req"), "expert"),
        P(("group", "req")),
        P("req", "expert"),
        P("expert"),
        P("req", "expert"),
        P("req", "expert"),
        P("expert", "req"),
    )
    out_specs = (P(("group", "expert"), "req"), P(("group", "req"), "expert"))
    return jax.shard_map(
        per_device, mesh=mesh, in_specs=in_specs, out_specs=out_specs, check_vma=False
    )
```

profile of v0, /device:TPU:25, one launch (start us, length us, event | category | flops | bytes accessed | tf_op | source)
XLA Modules:
  0.0 376.1 jit_solution(8400339418862169290)
XLA Ops:
  7.2 0.0 copy-start
  7.2 0.0 reduce-scatter.2.cloned.1.call-start
  7.3 0.7 convert_element_type.26
  8.0 0.7 compare_and_fusion
  8.7 0.7 pad_maximum_fusion.1
  9.4 0.1 copy.20
  9.5 39.5 %copy.21.moe_gate_ref = bf16[8,4096,448]{2,1,0:T(8,128)(2,1)} copy(bf16[8,4096,448]{1,2,0:T(8,128)(2,1)} %param.17) | data formatting | bytes 58720256 | tf_op args[3]
  49.0 39.5 %copy.22.moe_up_ref = bf16[8,4096,448]{2,1,0:T(8,128)(2,1)} copy(bf16[8,4096,448]{1,2,0:T(8,128)(2,1)} %param.18) | data formatting | bytes 58720256 | tf_op args[4]
  88.6 0.6 pad.4.routes_ref
  89.2 0.0 copy-done
  89.2 1.2 gather_fusion
  90.3 0.0 copy-done.12
  90.4 1.1 broadcast_select_fusion.9
  91.5 204.7 %front.1 = (f32[256,1024]{1,0:T(8,128)}, bf16[16,1024]{1,0:T(8,128)(2,1)}, f32[4,8,128]{2,1,0:T(8,128)}, bf16[4,256,1024]{2,1,0:T(8,128)(2,1)}, bf16[1024,1792]{...) custom-call(bf16[256,1024]{1,0:T(8,128)(2,1)} %get-tuple-element.35., ...), custom_call_target="tpu_custom_call" | custom-call | tf_op jit(solution)/shard_map/front/pallas_call | solution.py:459
  296.2 0.0 copy-done.2
  296.2 0.0 copy-start.3
  296.2 0.0 copy-start.9
  296.2 3.6 fusion.10
  299.8 0.0 copy-done.3
  299.8 0.0 copy-done.9
  299.8 2.4 fusion.12
  302.1 0.0 copy-start.8
  302.2 0.0 copy-start.10
  302.2 3.9 %convolution_add_fusion.2 = f32[256,1792]{1,0:T(8,128)S(1)} fusion(f32[256,1792]{1,0:T(8,128)} %fusion.10, bf16[1024,1792]{1,0:T(8,128)(2,1)} %get-tuple-element.22, bf16[4,256,1024]{2,1,0:T(8,128)(2,1)S(1)} %copy-done.9, s32[]{:T(128)S(6)} %select_n.92), kind=kOutput, calls=%fused_computation.5 | convolution fusion | flops 939982848 | bytes 7864324 | tf_op jit(solution)/shard_map/dot_general | solution.py:532
  306.1 0.3 copy-done.10
  306.4 1.1 convolution_add_fusion.5
  307.6 0.9 copy-done.7
  308.4 1.1 convolution_add_fusion.1
  309.6 0.9 copy-done.6
  310.5 1.1 convolution_add_fusion.4
  311.6 0.9 copy-done.5
  312.5 1.2 fusion.2
  313.7 0.9 copy-done.18
  314.6 1.3 fusion.3
  315.9 0.7 copy-done.17
  316.6 1.4 convolution_convert_fusion
  318.0 0.7 copy-done.16
  318.6 1.1 convolution_convert_fusion.1
  319.8 0.9 copy-done.15
  320.7 1.2 convolution_convert_fusion.2
  321.9 0.9 copy-done.4
  322.7 1.2 broadcast_select_fusion.8
  324.0 1.5 pad_maximum_fusion
  325.5 0.0 reduce-scatter.2.cloned.1.call-update
  325.5 41.1 %reduce-scatter.2.cloned.1.call-done = bf16[256,1024]{1,0:T(8,128)(2,1)} async-done(((bf16[256,4096]{1,0:T(8,128)(2,1)}), bf16[256,1024]{1,0:T(8,128)(2,1)}) %reduce-scatter.2.cloned.1.call-update) | async-done | bytes 524304 | tf_op jit(solution)/shard_map/reduce_scatter | solution.py:545
  366.6 2.0 add_convert_fusion
  368.6 0.6 copy.24
  369.2 0.0 copy-done.1
  (21 shorter events, 0.1 us)
Async XLA Ops:
  7.2 82.0 %copy-start = (bf16[256,1024]{1,0:T(8,128)(2,1)S(1)}, bf16[256,1024]{1,0:T(8,128)(2,1)}, u32[]{:S(2)}) copy-start(bf16[256,1024]{1,0:T(8,128)(2,1)} %param.21) | copy-start | bytes 1572868
  7.2 359.5 %reduce-scatter.2.cloned.1.call-start = ((), (), s32[]{:S(2)}) async-start(), calls=%async_computation.1 | async-start | bytes 2621440 | tf_op jit(solution)/shard_map/reduce_scatter | solution.py:545
  89.2 1.2 copy-start.12
  91.5 204.7 %copy-start.2 = (bf16[1024,1792]{1,0:T(8,128)(2,1)S(1)}, bf16[1024,1792]{1,0:T(8,128)(2,1)}, u32[]{:S(2)}) copy-start(bf16[1024,1792]{1,0:T(8,128)(2,1)} %up_ref.1) | copy-start | bytes 11010052
  296.2 3.6 copy-start.3
  296.2 3.6 copy-start.9
  299.8 2.4 copy-start.14
  302.1 3.9 %copy-start.8 = (bf16[1024,1792]{1,0:T(8,128)(2,1)S(1)}, bf16[1024,1792]{1,0:T(8,128)(2,1)}, u32[]{:S(2)}) copy-start(bf16[1024,1792]{1,0:T(8,128)(2,1)} %get-tuple-element.19) | copy-start | bytes 11010052
  302.2 4.2 %copy-start.10 = (f32[256,1792]{1,0:T(8,128)S(1)}, f32[256,1792]{1,0:T(8,128)}, u32[]{:S(2)}) copy-start(f32[256,1792]{1,0:T(8,128)} %fusion.12) | copy-start | bytes 5505028
  306.4 2.0 copy-start.7
  308.4 2.0 copy-start.6
  310.5 2.0 copy-start.5
  312.5 2.0 copy-start.18
  314.6 2.0 copy-start.17
  316.6 2.0 copy-start.16
  318.6 2.0 copy-start.15
  320.7 2.0 copy-start.4
  325.5 41.2 %copy-start.11 = (f32[256,1024]{1,0:T(8,128)S(1)}, f32[256,1024]{1,0:T(8,128)}, u32[]{:S(2)}) copy-start(f32[256,1024]{1,0:T(8,128)} %get-tuple-element.16) | copy-start | bytes 3145732
  325.5 43.8 %copy-start.1 = (bf16[256,1024]{1,0:T(8,128)(2,1)S(1)}, bf16[256,1024]{1,0:T(8,128)(2,1)}, u32[]{:S(2)}) copy-start(bf16[256,1024]{1,0:T(8,128)(2,1)} %param.21) | copy-start | bytes 1572868
  325.5 43.1 %copy-start.13 = (bf16[16,1024]{1,0:T(8,128)(2,1)S(1)}, bf16[16,1024]{1,0:T(8,128)(2,1)}, u32[]{:S(2)}) copy-start(bf16[16,1024]{1,0:T(8,128)(2,1)} %get-tuple-element.38) | copy-start | bytes 98308
Sparse Core Ops, SparseCore 0:
  325.6 40.9 reduce-scatter.1
where the time goes:
time: 382 us; the launch traced here: 376 us
  Pallas kernels  205 us (54%)
  local copies, waits for them, and re-layouts  88.6 us (23%)
  waiting for transfers between devices  41.1 us (11%)
  matrix products  20.6 us (5%)
  between operations  14.3 us (4%)
  other arithmetic  6.73 us (2%)
    pallas_call x1, Pallas kernels, front(): pl.pallas_call(functools.partial(front_kernel, (n_expert, n_req, n_group,...  205 us
    unnamed x41, local copies, waits for them, and re-layouts  86.8 us
    reduce_scatter x1, waiting for transfers between devices, fused(): mlp_sum = lax.psum_scatter(terms, 'expert', scatter_dimension=1, tiled=True)  41.1 us
    dot_general x8, matrix products, project(): jnp.dot(c, w, preferred_element_type=jnp.float32)  15.7 us
  transfers between devices with their start and end apart: 1, of which 1 were waited for; matrix products, arithmetic and copies ran while one was open for 0% of the time, Pallas kernels for 0%

commit v1 on v0

--- a/solution.py
+++ b/solution.py
@@ -9,6 +9,8 @@
 
 EXPERTS = 8
 EPS = 1e-05
+CUTS = 4
+AHEAD = 4
 
 
 def verify_layer(verify_in, expert_ids, gate_weights, moe_gate, moe_up, moe_down):
@@ -146,16 +148,17 @@
     return (joined_state + mlp_sum.astype(jnp.float32)).astype(jnp.bfloat16)
 
 
-def front_kernel(
+def whole_kernel(
     shape,
     mine_ref, theirs_ref, gain_ref, rows_ref, routes_ref,
     join_ref, gate_ref, up_ref, down_ref, moe_gate_ref, moe_up_ref, moe_down_ref,
-    state_ref, verify_ref, squares_ref, scaled_ref,
+    verify_ref, out_ref,
     gate_sib, up_sib, down_sib, gate_far, up_far, down_far, gate_sibfar, up_sibfar, down_sibfar,
     near_all, far_all, near_acc, sent_acc, swap_out, swap_in, join_all, square_buf, scaled_buf,
     row_all, route_all, gate_buf, up_buf, down_buf, moe_acc, moe_out, moe_in, merged_out, merged_in,
     ring_send_r, ring_send_l, ring_recv, misc_send, misc_recv, local_sem, moe_sem,
     mate_send, mate_recv, wide_send, wide_recv,
+    gate_acc, up_acc, hidden_buf, sum_in, stream_sem, sum_send, sum_recv,
 ):
     n_expert, n_req, n_group, slices = shape
     half = n_req // 2
@@ -270,7 +273,7 @@
         sib_out.append(c)
 
     weights = ((gate_ref, gate_far, gate_sibfar), (up_ref, up_far, up_sibfar), (down_ref, down_far, down_sibfar))
-    cuts = 2
+    cuts = CUTS
     chunks = []
     for own, far, sibfar in weights:
         part = own.shape[0] // n_group
@@ -298,8 +301,8 @@
 
     def relay(c):
         over_req(c).wait_recv()
-        if c + 2 < count:
-            over_req(c + 2).start()
+        if c + AHEAD < count:
+            over_req(c + AHEAD).start()
         over_group(c).start()
         to_sib(c, 2).start()
         if c > 0:
@@ -311,14 +314,21 @@
 
     cross.wait_recv()
     ring_start(1, far_all)
-    over_req(0).start()
-    over_req(1).start()
+    for c in range(AHEAD):
+        over_req(c).start()
     ring_step(0, near_all, 1)
     for c in rows_exp + routes_out:
         c.wait_recv()
     moe_acc[...] = jnp.zeros_like(moe_acc)
     own_rows = rows_ref.shape[0]
     rows = own_rows * n_expert
+
+    def tiled(width, size, body):
+        def step(n, carry):
+            body(pl.ds(pl.multiple_of(n * size, size), size))
+            return carry
+
+        lax.fori_loop(0, width // size, step, 0)
 
     def expert_piece(k, carry):
         slot = lax.rem(k, 2)
@@ -335,10 +345,15 @@
         expert = ((e * local + k) // slices).astype(jnp.float32)
         mixing = jnp.where(routes[:, 0:1] == expert, routes[:, 2:3], 0.0)
         mixing += jnp.where(routes[:, 1:2] == expert, routes[:, 3:4], 0.0)
-        a = jnp.dot(x, gate_buf[slot], preferred_element_type=jnp.float32)
-        b = jnp.dot(x, up_buf[slot], preferred_element_type=jnp.float32)
+        last = (((1,), (1,)), ((), ()))
+        a = lax.dot_general(x, gate_buf[slot], last, preferred_element_type=jnp.float32)
+        b = lax.dot_general(x, up_buf[slot], last, preferred_element_type=jnp.float32)
         hidden = (a / (1.0 + jnp.exp(-a)) * b * mixing).astype(jnp.bfloat16)
-        moe_acc[...] += jnp.dot(hidden, down_buf[slot], preferred_element_type=jnp.float32)
+
+        def columns(at):
+            moe_acc[:, at] += jnp.dot(hidden, down_buf[slot, :, at], preferred_element_type=jnp.float32)
+
+        tiled(row_all.shape[2], 512, columns)
         return carry
 
     def moe(start, stop):
@@ -352,9 +367,10 @@
     relay(0)
     ring_step(0, near_all, 3)
     moe(2 * quarter, 3 * quarter)
+    relay(1)
     ring_step(1, far_all, 2)
     moe(3 * quarter, local)
-    relay(1)
+    relay(2)
 
     moe_out[...] = moe_acc[...].astype(jnp.bfloat16).reshape(moe_out.shape)
     merge_exp = mates(lambda m: moe_out.at[m], moe_in.at[e], 3, "expert", e, n_expert)
@@ -366,21 +382,25 @@
     tile = 256
 
     def join(buf, acc):
-        for n in range(acc.shape[1] // tile):
-            at = pl.ds(n * tile, tile)
+        def columns(at):
             total = 0.0
             for b in range(n_expert):
                 w = join_all[b // per, pl.ds(b % per * block, block), at]
                 total += jnp.dot(buf[b], w, preferred_element_type=jnp.float32)
             acc[:, at] = total
 
+        tiled(acc.shape[1], tile, columns)
+
+    relay(3)
     join(near_all, near_acc)
+    relay(4)
     ring_step(1, far_all, 3)
     join(far_all, sent_acc)
     swap_out[...] = sent_acc[...].astype(jnp.bfloat16)
     swap = remote(swap_out, swap_in, misc_send.at[5], misc_recv.at[5], req=partner)
     swap.start()
 
+    relay(5)
     for c in merge_exp:
         c.wait_recv()
     merged = moe_out[e].astype(jnp.float32)
@@ -391,14 +411,18 @@
     merge_req = mates(lambda m: merged_out.at[m], merged_in.at[r], 4, "req", r, n_req)
 
     swap.wait_recv()
-    state = near_acc[...] + swap_in[...].astype(jnp.float32)
-    state_ref[...] = state
-    scaled_buf[e] = (state * gain_ref[...]).astype(jnp.bfloat16)
+    height = near_acc.shape[0]
+    sums = jnp.zeros((height, 1), jnp.float32)
+    for n in range(block // tile):
+        at = pl.ds(n * tile, tile)
+        state = near_acc[:, at] + swap_in[:, at].astype(jnp.float32)
+        near_acc[:, at] = state
+        scaled_buf[e, :, at] = (state * gain_ref[:, at]).astype(jnp.bfloat16)
+        sums += jnp.sum(state * state, axis=1, keepdims=True)
     ring_start(2, scaled_buf)
     lane = lax.broadcasted_iota(jnp.int32, (128, 128), 1)
     line = lax.broadcasted_iota(jnp.int32, (128, 128), 0)
-    sums = jnp.sum(state * state, axis=1, keepdims=True)
-    for j in range(state.shape[0] // 128):
+    for j in range(height // 128):
         picked = jnp.where(lane == line, sums[j * 128:(j + 1) * 128], 0.0)
         square_buf[e, j:j + 1, :] = jnp.sum(picked, axis=0, keepdims=True)
     squares_out = mates(lambda m: square_buf.at[e], square_buf.at[e], 5, "expert", e, n_expert)
@@ -410,34 +434,184 @@
         out += merged_in[lax.rem(r + n_req - s, n_req)].astype(jnp.float32)
     verify_ref[...] = out.astype(jnp.bfloat16)
 
-    relay(2)
+    relay(6)
     ring_step(2, scaled_buf, 1)
-    relay(3)
+    relay(7)
     ring_step(2, scaled_buf, 2)
-    relay(4)
+    relay(8)
     ring_step(2, scaled_buf, 3)
     for c in squares_out:
         c.wait_recv()
-    squares_ref[...] = square_buf[...]
-    keep = pltpu.make_async_copy(scaled_buf, scaled_ref, local_sem.at[1])
-    keep.start()
-    relay(5)
+    total = square_buf[0]
+    for b in range(1, n_expert):
+        total += square_buf[b]
+    spread = [
+        jnp.sum(jnp.where(lane == line, total[j:j + 1], 0.0), axis=1, keepdims=True)
+        for j in range(height // 128)
+    ]
+    width = block * n_expert
+    scale = lax.rsqrt(jnp.concatenate(spread, axis=0) / width + EPS)
+
+    sibfar = lax.rem(sib + half, n_req)
+    piece_rows, wide = 256, gate_ref.shape[1]
+    steps = gate_ref.shape[0] // (2 * piece_rows)
+    homes = ((r, gate_ref, up_ref, down_ref), (sib, gate_sib, up_sib, down_sib),
+             (partner, gate_far, up_far, down_far), (sibfar, gate_sibfar, up_sibfar, down_sibfar))
+
+    def project_fetch(t):
+        home, slot = homes[t // steps], t % 2
+        copies = []
+        for w, buf in ((home[1], gate_buf), (home[2], up_buf)):
+            for q in range(2):
+                rows_at = pl.ds((t % steps * 2 + q) * piece_rows, piece_rows)
+                copies.append(pltpu.make_async_copy(
+                    w.at[rows_at], buf.at[slot, pl.ds(0, piece_rows), pl.ds(q * 2048, wide)],
+                    stream_sem.at[slot, len(copies)]))
+        return copies
+
+    def start(copies):
+        for c in copies:
+            c.start()
+
+    def project(first, stop):
+        start(project_fetch(first))
+        for t in range(first, stop):
+            if t + 1 < stop:
+                start(project_fetch(t + 1))
+            for c in project_fetch(t):
+                c.wait()
+            slot, index = t % 2, homes[t // steps][0]
+            for buf, acc in ((gate_buf, gate_acc), (up_buf, up_acc)):
+                def columns(at, buf=buf, acc=acc, slot=slot, index=index, t=t):
+                    value = 0.0 if t == 0 else acc[:, at]
+                    for q in range(2):
+                        x = scaled_buf[index, :, pl.ds((t % steps * 2 + q) * piece_rows, piece_rows)]
+                        w = buf[slot, pl.ds(0, piece_rows), pl.ds(pl.multiple_of(q * 2048 + at.start, 256), at.size)]
+                        value += jnp.dot(x, w, preferred_element_type=jnp.float32)
+                    acc[:, at] = value
+
+                tiled(wide, 256, columns)
+
+    for c in sib_out:
+        c.wait_recv()
+    project(0, 2 * steps)
+    relay(9)
+    for c in range(2 * cuts):
+        to_sib(c, 2).wait_recv()
+        to_sib(c, 3).wait_recv()
+    project(2 * steps, 4 * steps)
+
+    def activate(at):
+        gate = gate_acc[:, at] * scale
+        value = gate / (1.0 + jnp.exp(-gate)) * (up_acc[:, at] * scale)
+        hidden_buf[:, at] = value.astype(jnp.bfloat16)
+
+    tiled(wide, 256, activate)
+    relay(10)
+
+    pieces = down_ref.shape[0] // piece_rows
+    ring_finish(0, near_all)
+
+    def down_fetch(t):
+        slot = t % 2
+        return [
+            pltpu.make_async_copy(
+                homes[t][3].at[pl.ds(q * piece_rows, piece_rows)],
+                (gate_buf, up_buf)[q // 4].at[slot, pl.ds(0, piece_rows), pl.ds(q % 4 * block, block)],
+                stream_sem.at[slot, q])
+            for q in range(pieces)
+        ]
+
+    def down(first, stop):
+        start(down_fetch(first))
+        for t in range(first, stop):
+            if t + 1 < stop:
+                start(down_fetch(t + 1))
+            for c in down_fetch(t):
+                c.wait()
+            def columns(at, t=t):
+                value = 0.0
+                for q in range(pieces):
+                    w = (gate_buf, up_buf)[q // 4][
+                        t % 2, pl.ds(0, piece_rows), pl.ds(pl.multiple_of(q % 4 * block + at.start, 256), at.size)]
+                    x = hidden_buf[:, pl.ds(q * piece_rows, piece_rows)]
+                    value += jnp.dot(x, w, preferred_element_type=jnp.float32)
+                near_all[homes[t][0], :, at] = value.astype(jnp.bfloat16)
+
+            tiled(block, 256, columns)
+
+    down(0, 2)
+    relay(11)
     relay_last(count - 1)
-    keep.wait()
+    for c in range(2 * cuts, count):
+        to_sib(c, 2).wait_recv()
+        to_sib(c, 3).wait_recv()
+    down(2, 4)
+
+    def sum_left(p):
+        return remote(near_all.at[p], sum_in.at[0, p], sum_send.at[0, p], sum_recv.at[0, p],
+                      expert=lax.rem(e + n_expert - 1, n_expert))
+
+    def sum_right(p):
+        return remote(near_all.at[p], sum_in.at[1, p], sum_send.at[1, p], sum_recv.at[1, p],
+                      expert=lax.rem(e + 1, n_expert))
+
+    def add(p, way):
+        both = near_all[p].astype(jnp.float32) + sum_in[way, p].astype(jnp.float32)
+        near_all[p] = both.astype(jnp.bfloat16)
+
+    for dist in range(n_expert - 1, 0, -1):
+        @pl.when(e >= dist)
+        def _():
+            @pl.when(e < n_expert - 1)
+            def _():
+                sum_left(e - dist).wait_recv()
+                add(e - dist, 0)
+
+            sum_left(e - dist).start()
+
+        @pl.when(e + dist < n_expert)
+        def _():
+            @pl.when(e > 0)
+            def _():
+                sum_right(e + dist).wait_recv()
+                add(e + dist, 1)
+
+            sum_right(e + dist).start()
+
+    sent_acc[...] = near_acc[...] + near_all[e].astype(jnp.float32)
+
+    @pl.when(e < n_expert - 1)
+    def _():
+        sum_left(e).wait_recv()
+        sent_acc[...] += sum_in[0, e].astype(jnp.float32)
+
+    @pl.when(e > 0)
+    def _():
+        sum_right(e).wait_recv()
+        sent_acc[...] += sum_in[1, e].astype(jnp.float32)
+
+    out_ref[...] = sent_acc[...].astype(jnp.bfloat16)
+    for dist in range(1, n_expert):
+        @pl.when(e >= dist)
+        def _():
+            sum_left(e - dist).wait_send()
+
+        @pl.when(e + dist < n_expert)
+        def _():
+            sum_right(e + dist).wait_send()
 
     for c in rows_req + routes_out + rows_exp + merge_exp + merge_req + squares_out + sib_out:
         c.wait_send()
     for c in (cross, join_out, swap):
         c.wait_send()
-    for c in sib_out:
-        c.wait_recv()
-    for i, buf in enumerate((near_all, far_all, scaled_buf)):
-        ring_finish(i, buf)
+    ring_finish(1, far_all)
+    ring_finish(2, scaled_buf)
     for c in range(count):
         over_req(c).wait_send()
         over_group(c).wait_send()
-        to_sib(c, 2).wait()
-        to_sib(c, 3).wait()
+        to_sib(c, 2).wait_send()
+        to_sib(c, 3).wait_send()
 
 
 def front(
@@ -445,7 +619,8 @@
     moe_gate, moe_up, moe_down,
 ):
     n_expert, n_req, n_group = (lax.axis_size(a) for a in ("expert", "req", "group"))
-    local, width, ff = moe_gate.shape
+    moe_gate, moe_up = moe_gate.transpose(0, 2, 1), moe_up.transpose(0, 2, 1)
+    local, ff, width = moe_gate.shape
     slices = local * n_expert // EXPERTS
     rows, block = mine.shape
     own_rows, own_width = verify_in.shape
@@ -454,19 +629,17 @@
     weights = (draft_gate, draft_up, draft_down)
     like = [jax.ShapeDtypeStruct(w.shape, w.dtype) for w in weights]
     dma = pltpu.SemaphoreType.DMA
-    n_chunks = 6
+    n_chunks = 3 * CUTS
     big = max(n_expert, n_req)
     return pl.pallas_call(
-        functools.partial(front_kernel, (n_expert, n_req, n_group, slices)),
+        functools.partial(whole_kernel, (n_expert, n_req, n_group, slices)),
         out_shape=[
-            jax.ShapeDtypeStruct((rows, block), f32),
             jax.ShapeDtypeStruct(verify_in.shape, bf),
-            jax.ShapeDtypeStruct((n_expert, 8, 128), f32),
-            jax.ShapeDtypeStruct((n_expert, rows, block), bf),
+            jax.ShapeDtypeStruct((rows, block), bf),
             *like, *like, *like,
         ],
         in_specs=[vmem] * 5 + [hbm] * 7,
-        out_specs=[vmem] * 3 + [hbm] * 10,
+        out_specs=[vmem] * 2 + [hbm] * 9,
         scratch_shapes=[
             pltpu.VMEM((n_expert, rows, block), bf),
             pltpu.VMEM((n_expert, rows, block), bf),
@@ -479,8 +652,8 @@
             pltpu.VMEM((n_expert, rows, block), bf),
             pltpu.VMEM((n_expert, own_rows, width), bf),
             pltpu.VMEM((n_expert, *routes.shape), f32),
-            pltpu.VMEM((2, width, ff), bf),
-            pltpu.VMEM((2, width, ff), bf),
+            pltpu.VMEM((2, ff, width), bf),
+            pltpu.VMEM((2, ff, width), bf),
             pltpu.VMEM((2, ff, width), bf),
             pltpu.VMEM((n_expert * own_rows, width), f32),
             pltpu.VMEM((n_expert, own_rows, width), bf),
@@ -490,11 +663,16 @@
             dma((3, n_expert)), dma((3, n_expert)), dma((3, n_expert)),
             dma((6,)), dma((6,)), dma((2,)), dma((3, 2)),
             dma((6, big)), dma((6, big)), dma((4, n_chunks)), dma((4, n_chunks)),
+            pltpu.VMEM((rows, draft_gate.shape[1]), f32),
+            pltpu.VMEM((rows, draft_gate.shape[1]), f32),
+            pltpu.VMEM((rows, draft_gate.shape[1]), bf),
+            pltpu.VMEM((2, n_expert, rows, block), bf),
+            dma((2, 8)), dma((2, n_expert)), dma((2, n_expert)),
         ],
         compiler_params=pltpu.CompilerParams(
-            collective_id=0, has_side_effects=True, vmem_limit_bytes=56 * 2**20
+            collective_id=0, has_side_effects=True, vmem_limit_bytes=58 * 2**20
         ),
-        name="front",
+        name="whole",
     )(mine, theirs, gain, verify_in, routes, join_weight, *weights, moe_gate, moe_up, moe_down)
 
 
@@ -504,46 +682,18 @@
 ):
     n_expert, n_req = lax.axis_size("expert"), lax.axis_size("req")
     r = lax.axis_index("req")
-    half = n_req // 2
-    side, place = r // half, r % half
-    rows, width = draft_emb.shape[0], draft_emb.shape[1] * n_expert
+    side = r // (n_req // 2)
+    rows = draft_emb.shape[0]
     feat = jnp.take(draft_feat, parents - r * rows, axis=0)
     mine = jnp.where(side == 0, draft_emb, feat)
     theirs = jnp.where(side == 0, feat, draft_emb)
     routes = jnp.concatenate([expert_ids.astype(jnp.float32), gate_weights], axis=1)
     routes = jnp.pad(routes, ((0, 0), (0, 128 - routes.shape[1])))
-    state, verify_out, squares, inputs, *moved = front(
+    verify_out, draft_out, *_ = front(
         mine, theirs, norm_gain[None, :], verify_in, routes, join_weight,
         draft_gate, draft_up, draft_down, moe_gate, moe_up, moe_down,
     )
-    squares = jnp.sum(squares, axis=0).reshape(-1)[:rows]
-    scale = lax.rsqrt(squares[:, None] / width + EPS)
-    sib, partner = side * half + (1 - place), (r + half) % n_req
-    sibfar = partner + 1 - 2 * place
-    places = (r, sib, partner, sibfar)
-    per_gate, per_up, per_down = (
-        [w, moved[i], moved[3 + i], moved[6 + i]]
-        for i, w in enumerate((draft_gate, draft_up, draft_down))
-    )
-    columns = [lax.dynamic_index_in_dim(inputs, p, 0, keepdims=False) for p in places]
-
-    def project(shards):
-        return scale * sum(
-            jnp.dot(c, w, preferred_element_type=jnp.float32) for c, w in zip(columns, shards)
-        )
-
-    hidden = (jax.nn.silu(project(per_gate)) * project(per_up)).astype(jnp.bfloat16)
-    near0, near1, far0, far1 = (
-        jnp.dot(hidden, w, preferred_element_type=jnp.float32).astype(jnp.bfloat16)
-        for w in per_down
-    )
-    n0, n1 = jnp.where(place == 0, near0, near1), jnp.where(place == 0, near1, near0)
-    f0, f1 = jnp.where(place == 0, far0, far1), jnp.where(place == 0, far1, far0)
-    first = jnp.where(side == 0, n0, f0), jnp.where(side == 0, n1, f1)
-    second = jnp.where(side == 0, f0, n0), jnp.where(side == 0, f1, n1)
-    terms = jnp.concatenate([*first, *second], axis=1)
-    mlp_sum = lax.psum_scatter(terms, "expert", scatter_dimension=1, tiled=True)
-    return (verify_out, (state + mlp_sum.astype(jnp.float32)).astype(jnp.bfloat16))
+    return verify_out, draft_out
 
 
 def per_device(
@@ -569,7 +719,10 @@
         and join_weight.shape[0] % block == 0 and draft_gate.shape[0] == block
         and block % 256 == 0 and draft_gate.shape[1] % 128 == 0
         and rows % 128 == 0 and rows <= 1024 and expert_ids.shape[1] == 2
-        and moe_gate.shape[0] % 4 == 0 and draft_down.shape[0] % 64 == 0
+        and draft_gate.shape[1] <= 2048 and draft_gate.shape[1] % 256 == 0 and draft_down.shape[1] == block == 1024
+        and draft_gate.shape[0] % 512 == 0 and draft_down.shape[0] % 256 == 0
+        and draft_down.shape[0] <= 2048 and moe_gate.shape[0] % 4 == 0
+        and moe_gate.shape[1] == 4096 and moe_gate.shape[2] >= 256
     )
     if fits:
         return fused(

time: 382 us -> 276 us (0.72)
  local copies, waits for them, and re-layouts: 88.6 us -> 5.12 us
  Pallas kernels: 205 us -> 262 us
  waiting for transfers between devices: 41.1 us -> 0 us
  matrix products: 20.6 us -> 0 us
  between operations: 14.3 us -> 0.69 us
    unnamed x41 -> x8, local copies, waits for them, and re-layouts: 86.8 us -> 3.26 us
    pallas_call x1, Pallas kernels: 205 us -> 262 us  [front(): pl.pallas_call(functools.partial(whole_kernel, (n_expert, n_req, n_group,...]
    reduce_scatter x1 -> x0, waiting for transfers between devices: 41.1 us -> none  [fused(): mlp_sum = lax.psum_scatter(terms, 'expert', scatter_dimension=1, tiled=True)]
    dot_general x12 -> x0, matrix products: 20.6 us -> none  [the longest x8 15.7 us: project(): jnp.dot(c, w, preferred_element_type=jnp.float32)]
  transfers between devices with their start and end apart: 1 -> 0, of which waited for: 1 -> 0; matrix products, arithmetic and copies ran while one was open for 0% -> 0% of each run, Pallas kernels for 0% -> 0%
where the time goes in v1:
time: 276 us; the launch traced here: 271 us
  Pallas kernels  262 us (95%)
  local copies, waits for them, and re-layouts  5.12 us (2%)
  other arithmetic  3.25 us (1%)
    pallas_call x1, Pallas kernels, front(): pl.pallas_call(functools.partial(whole_kernel, (n_expert, n_req, n_group,...  262 us

profile of v1, /device:TPU:25, one launch (start us, length us, event | category | flops | bytes accessed | tf_op | source)
XLA Modules:
  0.0 270.8 jit_solution(10098678538699499151)
XLA Ops:
  0.6 0.0 copy-start
  0.6 0.0 copy-start.2
  0.7 0.8 convert_element_type.5
  1.4 0.7 pad_maximum_fusion
  2.1 0.7 compare_and_fusion
  2.8 0.1 copy.18
  2.9 0.6 pad.4.routes_ref
  3.5 0.0 copy-done
  3.5 1.2 gather_fusion
  4.7 0.0 copy-done.2
  4.7 1.1 broadcast_select_fusion.1
  5.8 0.0 copy-start.1
  5.8 261.7 %whole.1 = (bf16[16,1024]{1,0:T(8,128)(2,1)}, bf16[256,1024]{1,0:T(8,128)(2,1)}, bf16[1024,1792]{1,0:T(8,128)(2,1)}, bf16[1024,1792]{1,0:T(8,128)(2,1)}, bf16[17...) custom-call(bf16[256,1024]{1,0:T(8,128)(2,1)} %get-tuple-element.9.m, ...), custom_call_target="tpu_custom_call" | custom-call | tf_op jit(solution)/shard_map/whole/pallas_call | solution.py:634
  267.5 1.4 copy.21
  268.9 1.9 copy.22
  270.8 0.0 copy-done.1
  (1 shorter events, 0.0 us)
Async XLA Ops:
  0.6 2.9 %copy-start = (bf16[256,1024]{1,0:T(8,128)(2,1)S(1)}, bf16[256,1024]{1,0:T(8,128)(2,1)}, u32[]{:S(2)}) copy-start(bf16[256,1024]{1,0:T(8,128)(2,1)} %param.21) | copy-start | bytes 1572868
  0.6 4.0 %copy-start.2 = (bf16[256,1024]{1,0:T(8,128)(2,1)S(1)}, bf16[256,1024]{1,0:T(8,128)(2,1)}, u32[]{:S(2)}) copy-start(bf16[256,1024]{1,0:T(8,128)(2,1)} %param.20) | copy-start | bytes 1572868
  5.8 265.0 %copy-start.1 = (bf16[256,1024]{1,0:T(8,128)(2,1)S(1)}, bf16[256,1024]{1,0:T(8,128)(2,1)}, u32[]{:S(2)}) copy-start(bf16[256,1024]{1,0:T(8,128)(2,1)} %param.21) | copy-start | bytes 1572868

commit v2 on v1

--- a/solution.py
+++ b/solution.py
@@ -10,7 +10,7 @@
 EXPERTS = 8
 EPS = 1e-05
 CUTS = 4
-AHEAD = 4
+AHEAD = 3
 
 
 def verify_layer(verify_in, expert_ids, gate_weights, moe_gate, moe_up, moe_down):
@@ -316,7 +316,6 @@
     ring_start(1, far_all)
     for c in range(AHEAD):
         over_req(c).start()
-    ring_step(0, near_all, 1)
     for c in rows_exp + routes_out:
         c.wait_recv()
     moe_acc[...] = jnp.zeros_like(moe_acc)
@@ -359,24 +358,6 @@
     def moe(start, stop):
         lax.fori_loop(start, stop, expert_piece, 0)
 
-    quarter = local // 4
-    moe(0, quarter)
-    ring_step(0, near_all, 2)
-    ring_step(1, far_all, 1)
-    moe(quarter, 2 * quarter)
-    relay(0)
-    ring_step(0, near_all, 3)
-    moe(2 * quarter, 3 * quarter)
-    relay(1)
-    ring_step(1, far_all, 2)
-    moe(3 * quarter, local)
-    relay(2)
-
-    moe_out[...] = moe_acc[...].astype(jnp.bfloat16).reshape(moe_out.shape)
-    merge_exp = mates(lambda m: moe_out.at[m], moe_in.at[e], 3, "expert", e, n_expert)
-
-    own_join.wait()
-    join_out.wait_recv()
     block = near_all.shape[2]
     per = join_ref.shape[0] // block
     tile = 256
@@ -391,24 +372,31 @@
 
         tiled(acc.shape[1], tile, columns)
 
-    relay(3)
-    join(near_all, near_acc)
-    relay(4)
+    quarter = local // 4
+    moe(0, quarter)
+    ring_step(1, far_all, 1)
+    relay(0)
+    moe(quarter, 2 * quarter)
+    ring_step(1, far_all, 2)
+    relay(1)
+    moe(2 * quarter, 3 * quarter)
     ring_step(1, far_all, 3)
+    ring_step(0, near_all, 1)
+    own_join.wait()
+    join_out.wait_recv()
     join(far_all, sent_acc)
     swap_out[...] = sent_acc[...].astype(jnp.bfloat16)
     swap = remote(swap_out, swap_in, misc_send.at[5], misc_recv.at[5], req=partner)
     swap.start()
-
-    relay(5)
-    for c in merge_exp:
-        c.wait_recv()
-    merged = moe_out[e].astype(jnp.float32)
-    for s in range(1, n_expert):
-        merged += moe_in[lax.rem(e + n_expert - s, n_expert)].astype(jnp.float32)
-    for j in range(n_req):
-        merged_out[j] = merged[:, j * own_width:(j + 1) * own_width].astype(jnp.bfloat16)
-    merge_req = mates(lambda m: merged_out.at[m], merged_in.at[r], 4, "req", r, n_req)
+    relay(2)
+    moe(3 * quarter, local)
+    ring_step(0, near_all, 2)
+    relay(3)
+
+    moe_out[...] = moe_acc[...].astype(jnp.bfloat16).reshape(moe_out.shape)
+    merge_exp = mates(lambda m: moe_out.at[m], moe_in.at[e], 3, "expert", e, n_expert)
+    ring_step(0, near_all, 3)
+    join(near_all, near_acc)
 
     swap.wait_recv()
     height = near_acc.shape[0]
@@ -427,6 +415,19 @@
         square_buf[e, j:j + 1, :] = jnp.sum(picked, axis=0, keepdims=True)
     squares_out = mates(lambda m: square_buf.at[e], square_buf.at[e], 5, "expert", e, n_expert)
 
+    relay(4)
+    for c in merge_exp:
+        c.wait_recv()
+    merged = moe_out[e].astype(jnp.float32)
+    for s in range(1, n_expert):
+        merged += moe_in[lax.rem(e + n_expert - s, n_expert)].astype(jnp.float32)
+    for j in range(n_req):
+        merged_out[j] = merged[:, j * own_width:(j + 1) * own_width].astype(jnp.bfloat16)
+    merge_req = mates(lambda m: merged_out.at[m], merged_in.at[r], 4, "req", r, n_req)
+
+    relay(5)
+    ring_step(2, scaled_buf, 1)
+    relay(6)
     for c in merge_req:
         c.wait_recv()
     out = merged_out[r].astype(jnp.float32)
@@ -434,12 +435,10 @@
         out += merged_in[lax.rem(r + n_req - s, n_req)].astype(jnp.float32)
     verify_ref[...] = out.astype(jnp.bfloat16)
 
-    relay(6)
-    ring_step(2, scaled_buf, 1)
+    ring_step(2, scaled_buf, 2)
     relay(7)
-    ring_step(2, scaled_buf, 2)
+    ring_step(2, scaled_buf, 3)
     relay(8)
-    ring_step(2, scaled_buf, 3)
     for c in squares_out:
         c.wait_recv()
     total = square_buf[0]
@@ -495,7 +494,6 @@
     for c in sib_out:
         c.wait_recv()
     project(0, 2 * steps)
-    relay(9)
     for c in range(2 * cuts):
         to_sib(c, 2).wait_recv()
         to_sib(c, 3).wait_recv()
@@ -507,7 +505,7 @@
         hidden_buf[:, at] = value.astype(jnp.bfloat16)
 
     tiled(wide, 256, activate)
-    relay(10)
+    relay(9)
 
     pieces = down_ref.shape[0] // piece_rows
     ring_finish(0, near_all)
@@ -540,44 +538,51 @@
 
             tiled(block, 256, columns)
 
+    def sum_left(p):
+        return remote(near_all.at[p], sum_in.at[0, p], sum_send.at[0, p], sum_recv.at[0, p],
+                      expert=lax.rem(e + n_expert - 1, n_expert))
+
+    def sum_right(p):
+        return remote(near_all.at[p], sum_in.at[1, p], sum_send.at[1, p], sum_recv.at[1, p],
+                      expert=lax.rem(e + 1, n_expert))
+
+    def add(p, way):
+        both = near_all[p].astype(jnp.float32) + sum_in[way, p].astype(jnp.float32)
+        near_all[p] = both.astype(jnp.bfloat16)
+
+    def pass_on(dist, of_side):
+        @pl.when((e >= dist) & ((e - dist) // half == of_side))
+        def _():
+            @pl.when(e < n_expert - 1)
+            def _():
+                sum_left(e - dist).wait_recv()
+                add(e - dist, 0)
+
+            sum_left(e - dist).start()
+
+        @pl.when((e + dist < n_expert) & ((e + dist) // half == of_side))
+        def _():
+            @pl.when(e > 0)
+            def _():
+                sum_right(e + dist).wait_recv()
+                add(e + dist, 1)
+
+            sum_right(e + dist).start()
+
+    side = r // half
     down(0, 2)
+    for dist in range(n_expert - 1, 0, -1):
+        pass_on(dist, side)
+        if dist == 2:
+            relay(10)
     relay(11)
     relay_last(count - 1)
     for c in range(2 * cuts, count):
         to_sib(c, 2).wait_recv()
         to_sib(c, 3).wait_recv()
     down(2, 4)
-
-    def sum_left(p):
-        return remote(near_all.at[p], sum_in.at[0, p], sum_send.at[0, p], sum_recv.at[0, p],
-                      expert=lax.rem(e + n_expert - 1, n_expert))
-
-    def sum_right(p):
-        return remote(near_all.at[p], sum_in.at[1, p], sum_send.at[1, p], sum_recv.at[1, p],
-                      expert=lax.rem(e + 1, n_expert))
-
-    def add(p, way):
-        both = near_all[p].astype(jnp.float32) + sum_in[way, p].astype(jnp.float32)
-        near_all[p] = both.astype(jnp.bfloat16)
-
     for dist in range(n_expert - 1, 0, -1):
-        @pl.when(e >= dist)
-        def _():
-            @pl.when(e < n_expert - 1)
-            def _():
-                sum_left(e - dist).wait_recv()
-                add(e - dist, 0)
-
-            sum_left(e - dist).start()
-
-        @pl.when(e + dist < n_expert)
-        def _():
-            @pl.when(e > 0)
-            def _():
-                sum_right(e + dist).wait_recv()
-                add(e + dist, 1)
-
-            sum_right(e + dist).start()
+        pass_on(dist, 1 - side)
 
     sent_acc[...] = near_acc[...] + near_all[e].astype(jnp.float32)
 

time: 276 us -> 258 us (0.935); the launches traced: 271 us -> 257 us
  Pallas kernels: 262 us -> 248 us
    pallas_call x1, Pallas kernels: 262 us -> 248 us  [front(): pl.pallas_call(functools.partial(whole_kernel, (n_expert, n_req, n_group,...]
where the time goes in v2:
time: 258 us; the launch traced here: 257 us
  Pallas kernels  248 us (96%)
  local copies, waits for them, and re-layouts  5.12 us (2%)
  other arithmetic  3.25 us (1%)
    pallas_call x1, Pallas kernels, front(): pl.pallas_call(functools.partial(whole_kernel, (n_expert, n_req, n_group,...  248 us

profile of v2, /device:TPU:25, one launch (start us, length us, event | category | flops | bytes accessed | tf_op | source)
XLA Modules:
  0.0 257.4 jit_solution(17149540012026921214)
XLA Ops:
  0.6 0.0 copy-start
  0.6 0.0 copy-start.2
  0.7 0.8 convert_element_type.5
  1.4 0.7 pad_maximum_fusion
  2.1 0.7 compare_and_fusion
  2.8 0.1 copy.18
  2.9 0.6 pad.4.routes_ref
  3.5 0.0 copy-done
  3.5 1.2 gather_fusion
  4.7 0.0 copy-done.2
  4.7 1.1 broadcast_select_fusion.1
  5.8 0.0 copy-start.1
  5.8 248.3 %whole.1 = (bf16[16,1024]{1,0:T(8,128)(2,1)}, bf16[256,1024]{1,0:T(8,128)(2,1)}, bf16[1024,1792]{1,0:T(8,128)(2,1)}, bf16[1024,1792]{1,0:T(8,128)(2,1)}, bf16[17...) custom-call(bf16[256,1024]{1,0:T(8,128)(2,1)} %get-tuple-element.9.m, ...), custom_call_target="tpu_custom_call" | custom-call | tf_op jit(solution)/shard_map/whole/pallas_call | solution.py:639
  254.1 1.4 copy.21
  255.5 1.9 copy.22
  257.4 0.0 copy-done.1
  (1 shorter events, 0.0 us)
Async XLA Ops:
  0.6 2.9 %copy-start = (bf16[256,1024]{1,0:T(8,128)(2,1)S(1)}, bf16[256,1024]{1,0:T(8,128)(2,1)}, u32[]{:S(2)}) copy-start(bf16[256,1024]{1,0:T(8,128)(2,1)} %param.21) | copy-start | bytes 1572868
  0.6 4.0 %copy-start.2 = (bf16[256,1024]{1,0:T(8,128)(2,1)S(1)}, bf16[256,1024]{1,0:T(8,128)(2,1)}, u32[]{:S(2)}) copy-start(bf16[256,1024]{1,0:T(8,128)(2,1)} %param.20) | copy-start | bytes 1572868
  5.8 251.6 %copy-start.1 = (bf16[256,1024]{1,0:T(8,128)(2,1)S(1)}, bf16[256,1024]{1,0:T(8,128)(2,1)}, u32[]{:S(2)}) copy-start(bf16[256,1024]{1,0:T(8,128)(2,1)} %param.21) | copy-start | bytes 1572868

commit v3 on v2

--- a/solution.py
+++ b/solution.py
@@ -10,7 +10,7 @@
 EXPERTS = 8
 EPS = 1e-05
 CUTS = 4
-AHEAD = 3
+AHEAD = 5
 
 
 def verify_layer(verify_in, expert_ids, gate_weights, moe_gate, moe_up, moe_down):

time: 258 us -> 268 us (1.039)
  Pallas kernels: 248 us -> 256 us
    pallas_call x1, Pallas kernels: 248 us -> 256 us  [front(): pl.pallas_call(functools.partial(whole_kernel, (n_expert, n_req, n_group,...]
where the time goes in v3:
time: 268 us; the launch traced here: 265 us
  Pallas kernels  256 us (96%)
  local copies, waits for them, and re-layouts  5.12 us (2%)
  other arithmetic  3.25 us (1%)
    pallas_call x1, Pallas kernels, front(): pl.pallas_call(functools.partial(whole_kernel, (n_expert, n_req, n_group,...  256 us

profile of v3, /device:TPU:25, one launch (start us, length us, event | category | flops | bytes accessed | tf_op | source)
XLA Modules:
  0.0 265.5 jit_solution(10494083732342254473)
XLA Ops:
  0.6 0.0 copy-start
  0.6 0.0 copy-start.2
  0.7 0.8 convert_element_type.5
  1.4 0.7 pad_maximum_fusion
  2.1 0.7 compare_and_fusion
  2.8 0.1 copy.18
  2.9 0.6 pad.4.routes_ref
  3.5 0.0 copy-done
  3.5 1.2 gather_fusion
  4.7 0.0 copy-done.2
  4.7 1.1 broadcast_select_fusion.1
  5.8 0.0 copy-start.1
  5.8 256.4 %whole.1 = (bf16[16,1024]{1,0:T(8,128)(2,1)}, bf16[256,1024]{1,0:T(8,128)(2,1)}, bf16[1024,1792]{1,0:T(8,128)(2,1)}, bf16[1024,1792]{1,0:T(8,128)(2,1)}, bf16[17...) custom-call(bf16[256,1024]{1,0:T(8,128)(2,1)} %get-tuple-element.9.m, ...), custom_call_target="tpu_custom_call" | custom-call | tf_op jit(solution)/shard_map/whole/pallas_call | solution.py:639
  262.2 1.4 copy.21
  263.6 1.9 copy.22
  265.5 0.0 copy-done.1
  (1 shorter events, 0.0 us)
Async XLA Ops:
  0.6 2.9 %copy-start = (bf16[256,1024]{1,0:T(8,128)(2,1)S(1)}, bf16[256,1024]{1,0:T(8,128)(2,1)}, u32[]{:S(2)}) copy-start(bf16[256,1024]{1,0:T(8,128)(2,1)} %param.21) | copy-start | bytes 1572868
  0.6 4.0 %copy-start.2 = (bf16[256,1024]{1,0:T(8,128)(2,1)S(1)}, bf16[256,1024]{1,0:T(8,128)(2,1)}, u32[]{:S(2)}) copy-start(bf16[256,1024]{1,0:T(8,128)(2,1)} %param.20) | copy-start | bytes 1572868
  5.8 259.7 %copy-start.1 = (bf16[256,1024]{1,0:T(8,128)(2,1)S(1)}, bf16[256,1024]{1,0:T(8,128)(2,1)}, u32[]{:S(2)}) copy-start(bf16[256,1024]{1,0:T(8,128)(2,1)} %param.21) | copy-start | bytes 1572868
